TPU v7x, 512 devices: a whole 4x4x16 slice. The times are simulated.
512 devices in a mesh: layer: 8 (over y, core), feat: 16 (over z_hi, x), width: 4 (over z_lo).
Axes of the slice: x: 4, y: 4, z: 16 (z_hi: 4, z_lo: 4; z = z_hi * 4 + z_lo), core: 2. Of those that a mesh axis runs over, the one named last changes fastest.
Arguments:
- resid: bfloat16 [2, 128, 2048], P(None, 'layer', 'width'), may hold values from -6 to 6
- enc_w: bfloat16 [2, 2048, 65536], P(None, 'width', ('layer', 'feat')), may hold values from -0.125 to 0.125
- enc_b: float32 [2, 65536], P(None, ('layer', 'feat')), may hold values from -3 to 3
- dec_w: float32 [3, 65536, 2048], P(None, ('layer', 'feat'), 'width'), may hold values from -0.09375 to 0.09375
- dec_b: float32 [2, 2048], P(None, 'width'), may hold values from -2 to 2
- target: float32 [2, 128, 2048], P(None, ('layer', 'feat'), 'width'), may hold values from -6 to 6
Outputs:
- recon: float32 [2, 128, 2048], P(None, ('layer', 'feat'), 'width')
- err: float32 [2, 128], P(None, ('layer', 'feat'))
All inputs are finite; a program needn't handle non-finite values.
Results may differ from a plain program's by a relative error of at most 0.00035.
Values may be sent and summed in bfloat16 or wider, within the bound.
A program may use at most 64 MiB of HBM per device.

v0:
```python
import jax
import jax.numpy as jnp
from jax import lax
from jax.sharding import PartitionSpec as P


def decode_rows(act, dec_w, target_idx):
    total = None
    for layer_idx in range(target_idx + 1):
        block = target_idx * (target_idx + 1) // 2 + layer_idx
        rows = act[layer_idx]
        term = jnp.dot(
            rows, dec_w[block], precision=lax.Precision.HIGHEST, preferred_element_type=jnp.float32
        )
        total = term if total is None else total + term
    return total


def per_device(resid, enc_w, enc_b, dec_w, dec_b, target):
    layers = resid.shape[0]
    gathered = lax.all_gather(resid, "layer", axis=1, tiled=True)
    tokens = gathered.shape[1]
    partial_pre = jnp.einsum("ltd,ldf->ltf", gathered, enc_w, preferred_element_type=jnp.float32)
    pre = lax.psum(partial_pre, "width")
    act = jnp.maximum(pre + enc_b[:, None, :], 0.0)
    own_rows = tokens // lax.axis_size(("layer", "feat"))
    pieces = []
    for target_idx in range(layers):

        def decode_single(start, count, target_idx=target_idx):
            return decode_rows(act, dec_w, target_idx)

        pieces.append(
            lax.psum_scatter(
                decode_single(jnp.int32(0), own_rows * lax.axis_size(("layer", "feat"))),
                ("layer", "feat"),
                scatter_dimension=0,
                tiled=True,
            )
        )
    summed = jnp.stack(pieces, 0)
    recon = summed + dec_b[:, None, :]
    diff = recon - target
    sq_error, sq_target = lax.psum(
        (jnp.sum(diff * diff, axis=2), jnp.sum(target * target, axis=2)), "width"
    )
    err = sq_error / (sq_target + 1e-06)
    return (recon, err)


def solution(mesh):
    in_specs = (
        P(None, "layer", "width"),
        P(None, "width", ("layer", "feat")),
        P(None, ("layer", "feat")),
        P(None, ("layer", "feat"), "width"),
        P(None, "width"),
        P(None, ("layer", "feat"), "width"),
    )
    out_specs = (P(None, ("layer", "feat"), "width"), P(None, ("layer", "feat")))
    return jax.shard_map(
        per_device, mesh=mesh, in_specs=in_specs, out_specs=out_specs, check_vma=False
    )
```

profile of v0, /device:TPU:1, one launch (start us, length us, event | category | flops | bytes accessed | tf_op | source)
XLA Modules:
  0.0 1566.3 jit_solution(10520074433764686368)
XLA Ops:
  7.2 0.0 copy-start
  7.2 0.0 all-reduce.7.cloned.1.call-start
  7.2 19.9 %all_gather.3 = bf16[2,128,512]{2,1,0:T(8,128)(2,1)S(1)} all-gather(bf16[2,16,512]{2,1,0:T(8,128)(2,1)} %param.6), channel_id=1, replica_groups=mesh['layer'=8,'feat'=16,'width'=4] {'layer'}, dimensions={1}, use_global_device_ids=true | all-gather | bytes 294912 | tf_op jit(solution)/shard_map/all_gather | solution.py:21
  27.1 0.0 copy-done
  27.1 1.1 fusion.12
  28.2 0.0 all-reduce.7.cloned.1.call-update
  28.3 0.0 copy-start.1
  28.3 0.0 copy-start.2
  28.3 0.0 all-reduce.9.cloned.1.call-start
  28.3 58.7 %all-reduce.7.cloned.1.call-done = f32[2,128,512]{2,1,0:T(8,128)} async-done(((f32[2,128,512]{2,1,0:T(8,128)}), f32[2,128,512]{2,1,0:T(8,128)}) %all-reduce.7.cloned.1.call-update) | async-done | bytes 524304 | tf_op jit(solution)/shard_map/psum | solution.py:24
  87.1 1.1 add_maximum_fusion
  88.2 1.9 fusion.1
  90.1 2.7 fusion.3
  92.8 2.6 convolution_add_fusion
  95.4 0.0 all-reduce.9.cloned.1.call-update
  95.4 1.3 dynamic-slice
  96.7 0.0 copy-done.1
  96.7 0.1 multiply_reduce_fusion
  96.8 1452.0 %all-reduce.9.cloned.1.call-done = (f32[128,512]{1,0:T(8,128)}, f32[128,512]{1,0:T(8,128)}) async-done(((f32[128,512]{1,0:T(8,128)}, f32[128,512]{1,0:T(8,128)}), (f32[128,512]{1,0:T(8,128)}, f32[128,512]{1,0:T(8,128)})) %all-reduce.9.cloned.1.call-update) | async-done | bytes 524304
  1548.9 1.4 constant_dynamic-slice_fusion
  1550.3 0.0 copy-done.2
  1550.3 0.1 fusion.10
  1550.4 0.6 copy.11
  1551.0 7.9 all-reduce.3
  1558.9 0.5 add_divide_fusion
Async XLA Ops:
  7.2 20.0 %copy-start = (bf16[2,512,512]{2,1,0:T(8,128)(2,1)S(1)}, bf16[2,512,512]{2,1,0:T(8,128)(2,1)}, u32[]{:S(2)}) copy-start(bf16[2,512,512]{2,1,0:T(8,128)(2,1)} %param.7) | copy-start | bytes 3145732
  7.2 79.9 %all-reduce.7.cloned.1.call-start = ((), (), s32[]{:S(2)}) async-start(), calls=%async_computation | async-start | bytes 1048576 | tf_op jit(solution)/shard_map/psum | solution.py:24
  28.3 68.4 %copy-start.1 = (f32[2,1,512]{2,1,0:T(1,128)S(1)}, f32[2,1,512]{2,1,0:T(1,128)}, u32[]{:S(2)}) copy-start(f32[2,1,512]{2,1,0:T(1,128)} %param.11) | copy-start | bytes 12292
  28.3 1522.0 %copy-start.2 = (f32[2,512]{1,0:T(2,128)S(1)}, f32[2,512]{1,0:T(2,128)}, u32[]{:S(2)}) copy-start(f32[2,512]{1,0:T(2,128)} %param.10) | copy-start | bytes 12292
  28.3 1520.6 %all-reduce.9.cloned.1.call-start = ((), (), s32[]{:S(2)}) async-start(), calls=%async_computation.1 | async-start | bytes 1048576
Sparse Core Ops, SparseCore 0:
  28.4 58.6 all-reduce.6
  95.6 1453.2 all-reduce.8
where the time goes:
time: 1590 us; the launch traced here: 1570 us
  waiting for transfers between devices  1510 us (95%)
  blocking collectives  27.8 us (2%)
    unnamed x3, waiting for transfers between devices  1450 us
    psum x1, waiting for transfers between devices, per_device(): pre = lax.psum(partial_pre, 'width')  58.7 us
  transfers between devices with their start and end apart: 2, of which 2 were waited for; matrix products, arithmetic and copies ran while one was open for 0% of the time, Pallas kernels for 0%

commit v1 on v0

v1 whole, which is shorter than its diff:
```python
import functools

import jax
import jax.numpy as jnp
from jax import lax
from jax.experimental import pallas as pl
from jax.experimental.pallas import tpu as pltpu
from jax.sharding import PartitionSpec as P

MESH = pl.DeviceIdType.MESH
F32 = jnp.float32
BF16 = jnp.bfloat16
CORES = 2
SIDE = 4
CHUNKS = 4


def block_of(target_idx, layer_idx):
    return target_idx * (target_idx + 1) // 2 + layer_idx


def kernel(
    layers,
    resid,
    enc_w,
    enc_b,
    dec_w,
    dec_b,
    target,
    recon,
    err,
    own_in,
    rows,
    ew,
    eb,
    dw,
    dw_hi,
    dw_lo,
    db,
    tg,
    part,
    heard,
    act,
    total,
    core_in,
    pair,
    plane_in,
    plane,
    deep_in,
    squares,
    in_sem,
    ew_sem,
    dw_sem,
    gather_sem,
    part_sem,
    act_sem,
    core_sem,
    plane_sem,
    own_sem,
    deep_sem,
    square_sem,
):
    me_layer = lax.axis_index("layer")
    me_feat = lax.axis_index("feat")
    me_width = lax.axis_index("width")
    y, core = me_layer // CORES, me_layer % CORES
    deep, x = me_feat // SIDE, me_feat % SIDE
    group = SIDE * CORES
    own_rows = own_in.shape[1]
    features = ew.shape[2]
    fc = features // CHUNKS
    width = dw.shape[2]
    steps = layers * CHUNKS

    is_mid = jnp.logical_and(me_width >= 1, me_width <= 2)
    is_end = jnp.logical_not(is_mid)
    kind = jnp.where(is_mid, 1, 0)
    forward = jnp.where(jnp.logical_or(me_width == 0, me_width == 2), 1, 2)
    outer = jnp.where(me_width == 1, 0, 3)

    local = [
        pltpu.make_async_copy(resid, own_in, in_sem.at[0]),
        pltpu.make_async_copy(enc_b, eb, in_sem.at[1]),
        pltpu.make_async_copy(dec_b, db, in_sem.at[2]),
        pltpu.make_async_copy(target, tg, in_sem.at[3]),
    ]
    enc_loads = [pltpu.make_async_copy(enc_w.at[l], ew.at[l], ew_sem.at[l]) for l in range(layers)]
    blocks = dw.shape[0]
    dec_loads = [pltpu.make_async_copy(dec_w.at[b], dw.at[b], dw_sem.at[b]) for b in range(blocks)]
    local[0].start()
    enc_loads[0].start()
    for copy in local[1:]:
        copy.start()
    for copy in dec_loads[: blocks - 1]:
        copy.start()
    for copy in enc_loads[1:]:
        copy.start()
    dec_loads[blocks - 1].start()

    barrier = pltpu.get_barrier_semaphore()

    def greet(layer, feat, wid):
        pl.semaphore_signal(barrier, inc=1, device_id=(layer, feat, wid), device_id_type=MESH)

    def greet_layer(d, carry):
        greet((me_layer + d) % group, me_feat, me_width)
        return carry

    def greet_plane(d, carry):
        to_y = (y + d // (SIDE - 1)) % SIDE
        to_x = (x + 1 + d % (SIDE - 1)) % SIDE
        greet(to_y * CORES + core, deep * SIDE + to_x, me_width)
        return carry

    def greet_deep(d, carry):
        greet(me_layer, ((deep + d) % SIDE) * SIDE + x, me_width)
        return carry

    def greet_width(d, carry):
        greet(me_layer, me_feat, (me_width + d) % SIDE)
        return carry

    lax.fori_loop(1, group, greet_layer, 0)
    lax.fori_loop(0, SIDE * (SIDE - 1), greet_plane, 0)
    lax.fori_loop(1, SIDE, greet_deep, 0)
    lax.fori_loop(1, SIDE, greet_width, 0)

    local[0].wait()
    place = lax.broadcasted_iota(jnp.int32, (own_rows, own_rows), 0)
    source = lax.broadcasted_iota(jnp.int32, (own_rows, own_rows), 1)
    swap = jnp.where(source == (place % SIDE) * SIDE + place // SIDE, 1.0, 0.0).astype(BF16)
    own = pl.ds(pl.multiple_of(me_layer * own_rows, own_rows), own_rows)
    for l in range(layers):
        swapped = jnp.dot(swap, own_in[l], preferred_element_type=F32)
        rows[l, own, :] = swapped.astype(BF16)

    pl.semaphore_wait(barrier, group - 1 + SIDE * (SIDE - 1) + 2 * (SIDE - 1))

    for l in range(layers):

        def push(d, carry, l=l):
            pltpu.make_async_remote_copy(
                src_ref=rows.at[l, own, :],
                dst_ref=rows.at[l, own, :],
                send_sem=gather_sem.at[0, l],
                recv_sem=gather_sem.at[1, l],
                device_id=((me_layer + d) % group, me_feat, me_width),
                device_id_type=MESH,
            ).start()
            return carry

        lax.fori_loop(1, group, push, 0)

    def gather_wait(way, l):
        some = rows.at[l, pl.ds(0, (group - 1) * own_rows), :]
        pltpu.make_async_copy(some, some, gather_sem.at[way, l]).wait()

    def split(b):
        dec_loads[b].wait()
        step = 64

        def body(i, carry):
            at = pl.ds(pl.multiple_of(i * step, step), step)
            whole = dw[b, at, :]
            high = whole.astype(BF16)
            dw_hi[b, at, :] = high
            dw_lo[b, at, :] = (whole - high.astype(F32)).astype(BF16)
            return carry

        lax.fori_loop(0, features // step, body, 0)

    for b in range(blocks - 1):
        split(b)

    def send_part(q):
        return pltpu.make_async_remote_copy(
            src_ref=part.at[q],
            dst_ref=heard.at[kind, q],
            send_sem=part_sem.at[0, kind, q],
            recv_sem=part_sem.at[1, kind, q],
            device_id=(me_layer, me_feat, forward),
            device_id_type=MESH,
        )

    def wait_part(k, q):
        pltpu.make_async_copy(heard.at[k, q], heard.at[k, q], part_sem.at[1, k, q]).wait()

    def send_act(q):
        return pltpu.make_async_remote_copy(
            src_ref=act.at[q],
            dst_ref=act.at[q],
            send_sem=act_sem.at[0, q],
            recv_sem=act_sem.at[1, q],
            device_id=(me_layer, me_feat, outer),
            device_id_type=MESH,
        )

    def encode(l):
        for h in range(CHUNKS):
            q = l * CHUNKS + h
            part[q] = jnp.dot(
                rows[l], ew[l, :, h * fc : (h + 1) * fc], preferred_element_type=F32
            )

            @pl.when(is_end)
            def _():
                send_part(q).start()

    def pass_on(q):
        @pl.when(is_mid)
        def _():
            wait_part(0, q)
            part[q] = part[q] + heard[0, q]
            send_part(q).start()

    def finish(q):
        l, h = divmod(q, CHUNKS)

        @pl.when(is_mid)
        def _():
            wait_part(1, q)
            bias = eb[l : l + 1, h * fc : (h + 1) * fc]
            act[q] = jnp.maximum(part[q] + heard[1, q] + bias, 0.0)
            send_act(q).start()

        @pl.when(is_end)
        def _():
            pltpu.make_async_copy(act.at[q], act.at[q], act_sem.at[1, q]).wait()

    def decode(q):
        l, h = divmod(q, CHUNKS)
        whole = act[q]
        high = whole.astype(BF16)
        low = (whole - high.astype(F32)).astype(BF16)
        for m in range(l, layers):
            b = block_of(m, l)
            w_hi = dw_hi[b, h * fc : (h + 1) * fc, :]
            w_lo = dw_lo[b, h * fc : (h + 1) * fc, :]
            term = jnp.dot(high, w_hi, preferred_element_type=F32)
            term += jnp.dot(low, w_hi, preferred_element_type=F32)
            term += jnp.dot(high, w_lo, preferred_element_type=F32)
            term = term.reshape(total.shape[1:])
            if q == 0:
                total[m] = term
            else:
                total[m] += term

    def send_core(m):
        return pltpu.make_async_remote_copy(
            src_ref=total.at[m, :, 1 - core],
            dst_ref=core_in.at[m],
            send_sem=core_sem.at[0, m],
            recv_sem=core_sem.at[1, m],
            device_id=(y * CORES + 1 - core, me_feat, me_width),
            device_id_type=MESH,
        )

    def own_plane(m):
        return pltpu.make_async_copy(pair.at[m, y * SIDE + x], plane_in.at[m, 0], own_sem.at[m])

    def send_plane(m, d):
        to_y, to_x = (y + d // SIDE) % SIDE, (x + d % SIDE) % SIDE
        return pltpu.make_async_remote_copy(
            src_ref=pair.at[m, to_y * SIDE + to_x],
            dst_ref=plane_in.at[m, d],
            send_sem=plane_sem.at[0, m],
            recv_sem=plane_sem.at[1, m],
            device_id=(to_y * CORES + core, deep * SIDE + to_x, me_width),
            device_id_type=MESH,
        )

    def plane_wait(way, m):
        some = plane_in.at[m, pl.ds(1, SIDE * SIDE - 1)]
        pltpu.make_async_copy(some, some, plane_sem.at[way, m]).wait()

    def send_deep(m, d):
        to = (deep + d) % SIDE
        return pltpu.make_async_remote_copy(
            src_ref=plane.at[m, to],
            dst_ref=deep_in.at[m, d],
            send_sem=deep_sem.at[0, m],
            recv_sem=deep_sem.at[1, m],
            device_id=(me_layer, to * SIDE + x, me_width),
            device_id_type=MESH,
        )

    def deep_wait(way, m):
        some = deep_in.at[m, pl.ds(1, SIDE - 1)]
        pltpu.make_async_copy(some, some, deep_sem.at[way, m]).wait()

    def start_plane(m):
        send_core(m).wait_recv()
        for to_y in range(SIDE):
            both = total[m, to_y, core] + core_in[m, to_y]
            for to_x in range(SIDE):
                pair[m, to_y * SIDE + to_x] = both[to_x * SIDE : (to_x + 1) * SIDE]
        own_plane(m).start()

        def body(d, carry):
            send_plane(m, d).start()
            return carry

        lax.fori_loop(1, SIDE * SIDE, body, 0)

    def start_deep(m):
        own_plane(m).wait()
        plane_wait(1, m)
        summed = jnp.sum(plane_in[m], axis=0)
        for to in range(SIDE):
            plane[m, to] = summed[to : to + 1]

        def body(d, carry):
            send_deep(m, d).start()
            return carry

        lax.fori_loop(1, SIDE, body, 0)

    def result(m):
        deep_wait(1, m)
        summed = plane[m, deep]
        for d in range(1, SIDE):
            summed = summed + deep_in[m, d]
        summed = summed + db[m : m + 1]
        recon[m] = summed
        diff = summed - tg[m]
        sq_error = jnp.sum(diff * diff, axis=1, keepdims=True)
        sq_target = jnp.sum(tg[m] * tg[m], axis=1, keepdims=True)
        lanes = squares.shape[2]
        squares[me_width, m : m + 1, :] = jnp.broadcast_to(sq_error, (1, lanes))
        squares[me_width, layers + m : layers + m + 1, :] = jnp.broadcast_to(sq_target, (1, lanes))

    gather_wait(1, 0)
    enc_loads[0].wait()
    encode(0)
    ahead = 2
    for q in range(ahead):
        pass_on(q)
    gather_wait(1, 1)
    enc_loads[1].wait()
    encode(1)
    split(blocks - 1)
    for copy in local[1:]:
        copy.wait()
    squares[me_width] = jnp.zeros(squares.shape[1:], F32)
    for q in range(steps):
        finish(q)
        if q + ahead < steps:
            pass_on(q + ahead)
        decode(q)
        if q == CHUNKS - 1:
            send_core(0).start()
        if q == CHUNKS:
            start_plane(0)
        if q == steps - 2:
            start_deep(0)
    send_core(1).start()
    result(0)
    start_plane(1)
    start_deep(1)
    result(1)

    def send_squares(d):
        return pltpu.make_async_remote_copy(
            src_ref=squares.at[me_width],
            dst_ref=squares.at[me_width],
            send_sem=square_sem.at[0, d],
            recv_sem=square_sem.at[1, d],
            device_id=(me_layer, me_feat, (me_width + d) % SIDE),
            device_id_type=MESH,
        )

    for d in range(1, SIDE):
        send_squares(d).start()
    for d in range(1, SIDE):
        send_squares(d).wait_recv()
    sums = jnp.sum(squares[...], axis=0)
    err[...] = sums[0:layers, 0:1] / (sums[layers : 2 * layers, 0:1] + 1e-06)

    for d in range(1, SIDE):
        send_squares(d).wait_send()
    for m in range(layers):
        gather_wait(0, m)
        send_core(m).wait_send()
        plane_wait(0, m)
        deep_wait(0, m)
    for q in range(steps):
        send_part(q).wait_send()

        @pl.when(is_mid)
        def _():
            send_act(q).wait_send()


def per_device(resid, enc_w, enc_b, dec_w, dec_b, target):
    layers, own_rows, wide = resid.shape
    features = enc_w.shape[2]
    blocks, _, width = dec_w.shape
    group = SIDE * CORES
    tokens = group * own_rows
    fc = features // CHUNKS
    steps = layers * CHUNKS
    vm = pltpu.VMEM
    dma = pltpu.SemaphoreType.DMA
    anywhere = pl.BlockSpec(memory_space=pl.ANY)
    in_vmem = pl.BlockSpec(memory_space=pltpu.VMEM)
    return pl.pallas_call(
        functools.partial(kernel, layers),
        out_shape=(
            jax.ShapeDtypeStruct((layers, 1, width), F32),
            jax.ShapeDtypeStruct((layers, 1), F32),
        ),
        in_specs=[anywhere] * 6,
        out_specs=(in_vmem, in_vmem),
        scratch_shapes=[
            vm((layers, own_rows, wide), BF16),
            vm((layers, tokens, wide), BF16),
            vm((layers, wide, features), BF16),
            vm((layers, features), F32),
            vm((blocks, features, width), F32),
            vm((blocks, features, width), BF16),
            vm((blocks, features, width), BF16),
            vm((layers, width), F32),
            vm((layers, 1, width), F32),
            vm((steps, tokens, fc), F32),
            vm((2, steps, tokens, fc), F32),
            vm((steps, tokens, fc), F32),
            vm((layers, SIDE, CORES, own_rows, width), F32),
            vm((layers, SIDE, own_rows, width), F32),
            vm((layers, SIDE * SIDE, SIDE, width), F32),
            vm((layers, SIDE * SIDE, SIDE, width), F32),
            vm((layers, SIDE, 1, width), F32),
            vm((layers, SIDE, 1, width), F32),
            vm((SIDE, 8, 128), F32),
            dma((4,)),
            dma((layers,)),
            dma((blocks,)),
            dma((2, layers)),
            dma((2, 2, steps)),
            dma((2, steps)),
            dma((2, layers)),
            dma((2, layers)),
            dma((layers,)),
            dma((2, layers)),
            dma((2, SIDE)),
        ],
        compiler_params=pltpu.CompilerParams(
            collective_id=0, has_side_effects=True, vmem_limit_bytes=48 * 1024 * 1024
        ),
        cost_estimate=pl.CostEstimate(
            flops=1_400_000_000, bytes_accessed=4_500_000, transcendentals=0
        ),
    )(resid, enc_w, enc_b, dec_w, dec_b, target)


def solution(mesh):
    in_specs = (
        P(None, "layer", "width"),
        P(None, "width", ("layer", "feat")),
        P(None, ("layer", "feat")),
        P(None, ("layer", "feat"), "width"),
        P(None, "width"),
        P(None, ("layer", "feat"), "width"),
    )
    out_specs = (P(None, ("layer", "feat"), "width"), P(None, ("layer", "feat")))
    return jax.shard_map(
        per_device, mesh=mesh, in_specs=in_specs, out_specs=out_specs, check_vma=False
    )
```

time: 1590 us -> 76.8 us (0.05)
  the two profiles are of different devices: /device:TPU:1 before, /device:TPU:4 now
where the time goes in v1:
time: 76.8 us; the launch traced here: 76.4 us
  Pallas kernels  68.6 us (89%)
  local copies, waits for them, and re-layouts  7.11 us (9%)
    pallas_call x1, Pallas kernels, per_device(): pl.pallas_call(functools.partial(kernel, layers), out_shape=(jax.ShapeDty...  68.6 us
    unnamed x13, local copies, waits for them, and re-layouts  6.52 us

profile of v1, /device:TPU:4, one launch (start us, length us, event | category | flops | bytes accessed | tf_op | source)
XLA Modules:
  0.0 76.4 jit_solution(1647275327883695372)
XLA Ops:
  0.6 0.0 copy-start
  0.6 1.9 %copy-done = f32[3,512,512]{2,1,0:T(8,128)S(1)} copy-done((f32[3,512,512]{2,1,0:T(8,128)S(1)}, f32[3,512,512]{2,1,0:T(8,128)}, u32[]{:S(2)}) %copy-start) | copy-done | bytes 3145752
  2.5 0.0 copy-start.1
  2.5 1.2 %copy-done.1 = bf16[2,512,512]{2,1,0:T(8,128)(2,1)S(1)} copy-done((bf16[2,512,512]{2,1,0:T(8,128)(2,1)S(1)}, bf16[2,512,512]{2,1,0:T(8,128)(2,1)}, u32[]{:S(2)}) %copy-start.1) | copy-done | bytes 1048600
  3.7 0.0 copy-start.2
  3.7 0.8 copy-done.2
  4.5 0.0 copy-start.3
  4.5 0.7 copy-done.3
  5.2 0.0 copy-start.4
  5.2 0.7 copy-done.4
  5.9 0.0 copy-start.5
  5.9 0.7 copy-done.5
  6.6 68.6 %shard_map.77 = (f32[2,1,512]{2,1,0:T(1,128)S(1)}, f32[2,1]{1,0:T(2,128)S(1)}) custom-call(bf16[2,16,512]{2,1,0:T(8,128)(2,1)S(1)} %copy-done.2, bf16[2,512,512]{2,1,0:T(8,128)(2,1)S(1)} %copy-done.1, f32[2,512]{1,0:T(2,128)S(1)} %copy-done.3, f32[3,512,512]{2,1,0:T(8,128)S(1)} %copy-done, f32[2,512]{1,0:T(2,128)S(1)} %copy-done.4, f32[2,1,512]{2,1,0:T(1,128)S(1)} %copy-done.5), custom_call_target="tpu_custom_call" | custom-call | flops 1400000000 | bytes 4500000 | tf_op jit(solution)/shard_map/pallas_call | solution.py:406
  75.2 0.6 copy.8
  75.8 0.6 copy.10
Async XLA Ops:
  0.6 1.9 %copy-start = (f32[3,512,512]{2,1,0:T(8,128)S(1)}, f32[3,512,512]{2,1,0:T(8,128)}, u32[]{:S(2)}) copy-start(f32[3,512,512]{2,1,0:T(8,128)} %dec_w.1) | copy-start | bytes 9437188
  2.5 1.2 %copy-start.1 = (bf16[2,512,512]{2,1,0:T(8,128)(2,1)S(1)}, bf16[2,512,512]{2,1,0:T(8,128)(2,1)}, u32[]{:S(2)}) copy-start(bf16[2,512,512]{2,1,0:T(8,128)(2,1)} %enc_w.1) | copy-start | bytes 3145732
  3.7 0.8 copy-start.2
  4.5 0.7 copy-start.3
  5.2 0.7 copy-start.4
  5.9 0.7 copy-start.5

commit v2 on v0

v2 whole, which is shorter than its diff:
```python
import functools

import jax
import jax.numpy as jnp
from jax import lax
from jax.experimental import pallas as pl
from jax.experimental.pallas import tpu as pltpu
from jax.sharding import PartitionSpec as P

MESH = pl.DeviceIdType.MESH
F32 = jnp.float32
BF16 = jnp.bfloat16
CORES = 2
SIDE = 4
SHIFTS = (0, 1, 3, 2)

WIRE = BF16
POWER = 12.0
BASE = 124.0
FINE = 2.0**-10


def to_wire(value):
    size = jnp.exp2(jnp.log2(jnp.abs(value) * (1.0 / FINE) + 1.0) * POWER - BASE)
    return jnp.where(value < 0.0, -size, size).astype(WIRE)


def from_wire(code):
    code = code.astype(F32)
    size = jnp.exp2((jnp.log2(jnp.abs(code)) + BASE) * (1.0 / POWER)) * FINE - FINE
    return jnp.where(code < 0.0, -size, size)


def block_of(target_idx, layer_idx):
    return target_idx * (target_idx + 1) // 2 + layer_idx


def kernel(
    layers,
    resid,
    enc_w,
    enc_b,
    dec_w,
    dec_b,
    target,
    recon,
    err,
    own_in,
    rows,
    ew,
    eb,
    dw,
    dw_hi,
    dw_lo,
    db,
    tg,
    part,
    outgoing,
    heard,
    act_wire,
    act,
    total,
    core_in,
    pair,
    plane_in,
    plane,
    deep_in,
    side,
    in_sem,
    ew_sem,
    dw_sem,
    gather_sem,
    part_sem,
    act_sem,
    core_sem,
    plane_sem,
    own_sem,
    deep_sem,
    side_sem,
    know_sem,
):
    me_layer = lax.axis_index("layer")
    me_feat = lax.axis_index("feat")
    me_width = lax.axis_index("width")
    y, core = me_layer // CORES, me_layer % CORES
    deep, x = me_feat // SIDE, me_feat % SIDE
    group = SIDE * CORES
    own_rows = own_in.shape[1]
    features = ew.shape[2]
    blocks = dw.shape[0]
    chunk_rows = CORES * own_rows

    is_low = me_width == 0
    is_high = me_width == SIDE - 1
    is_end = jnp.logical_or(is_low, is_high)
    is_mid = jnp.logical_not(is_end)
    kind = jnp.where(is_mid, 1, 0)
    forward = jnp.where(jnp.logical_or(me_width == 0, me_width == 2), 1, 2)
    outer = jnp.where(me_width == 1, 0, 3)
    beside = jnp.where(is_low, (deep + SIDE - 1) % SIDE, (deep + 1) % SIDE) * SIDE + x

    def signal(sem, layer, feat, wid):
        pl.semaphore_signal(sem, inc=1, device_id=(layer, feat, wid), device_id_type=MESH)

    barrier = pltpu.get_barrier_semaphore()

    def greet_layer(d, carry):
        signal(barrier, (me_layer + d) % group, me_feat, me_width)
        return carry

    def greet_others(d, carry):
        signal(barrier, me_layer, me_feat, (me_width + d) % SIDE)
        signal(barrier, me_layer, deep * SIDE + (x + d) % SIDE, me_width)
        return carry

    load_rows = pltpu.make_async_copy(resid, own_in, in_sem.at[0])
    load_rows.start()
    lax.fori_loop(1, group, greet_layer, 0)
    lax.fori_loop(1, SIDE, greet_others, 0)

    @pl.when(is_end)
    def _():
        signal(barrier, me_layer, beside, SIDE - 1 - me_width)

    load_bias = pltpu.make_async_copy(enc_b, eb, in_sem.at[1])
    load_db = pltpu.make_async_copy(dec_b, db, in_sem.at[2])
    load_tg = pltpu.make_async_copy(target, tg, in_sem.at[3])
    load_enc = [pltpu.make_async_copy(enc_w.at[l], ew.at[l], ew_sem.at[l]) for l in range(layers)]
    load_dec = [pltpu.make_async_copy(dec_w.at[b], dw.at[b], dw_sem.at[b]) for b in range(blocks)]
    for copy in load_enc + load_dec + [load_bias, load_db, load_tg]:
        copy.start()

    load_rows.wait()
    place = lax.broadcasted_iota(jnp.int32, (own_rows, own_rows), 0)
    source = lax.broadcasted_iota(jnp.int32, (own_rows, own_rows), 1)
    swap = jnp.where(source == (place % SIDE) * SIDE + place // SIDE, 1.0, 0.0).astype(BF16)
    for l in range(layers):
        swapped = jnp.dot(swap, own_in[l], preferred_element_type=F32)
        rows[me_layer, l] = swapped.astype(BF16)

    near = group - 1 + 2 * (SIDE - 1)
    pl.semaphore_wait(barrier, jnp.where(is_end, near + 1, near))

    def push(k, to_core):
        to = ((y + SHIFTS[k]) % SIDE) * CORES + to_core
        pltpu.make_async_remote_copy(
            src_ref=rows.at[me_layer],
            dst_ref=rows.at[me_layer],
            send_sem=gather_sem.at[0, 0],
            recv_sem=gather_sem.at[1, SHIFTS.index((SIDE - SHIFTS[k]) % SIDE)],
            device_id=(to, me_feat, me_width),
            device_id_type=MESH,
        ).start()

    push(0, 1 - core)
    for k in (3, 1, 2):
        push(k, core)
        push(k, 1 - core)

    def gather_wait(way, k, count):
        some = rows.at[pl.ds(0, count)]
        pltpu.make_async_copy(some, some, gather_sem.at[way, k]).wait()

    def greet_row(d, carry):
        signal(know_sem.at[4], me_layer, deep * SIDE + (x + d) % SIDE, me_width)
        return carry

    lax.fori_loop(1, SIDE, greet_row, 0)

    @pl.when(is_end)
    def _():
        signal(know_sem.at[0], me_layer, beside, SIDE - 1 - me_width)

    def know_lines(step):
        @pl.when(is_end)
        def _():
            pl.semaphore_wait(know_sem.at[step], 1)
            if step == 0:
                signal(know_sem.at[1], me_layer, me_feat, SIDE - 1 - me_width)
            elif step == 1:
                signal(know_sem.at[2], me_layer, beside, SIDE - 1 - me_width)
            else:
                signal(know_sem.at[3], me_layer, me_feat, forward)

    def split(b):
        load_dec[b].wait()
        step = 64

        def body(i, carry):
            at = pl.ds(pl.multiple_of(i * step, step), step)
            whole = dw[b, at, :]
            high = whole.astype(BF16)
            dw_hi[b, at, :] = high
            dw_lo[b, at, :] = (whole - high.astype(F32)).astype(BF16)
            return carry

        lax.fori_loop(0, features // step, body, 0)

    def send_part(k, l):
        return pltpu.make_async_remote_copy(
            src_ref=outgoing.at[k, l],
            dst_ref=heard.at[kind, k, l],
            send_sem=part_sem.at[0, k, l],
            recv_sem=part_sem.at[1 + kind, k, l],
            device_id=(me_layer, me_feat, forward),
            device_id_type=MESH,
        )

    def wait_part(which, k, l):
        some = heard.at[which, k, l]
        pltpu.make_async_copy(some, some, part_sem.at[1 + which, k, l]).wait()

    def send_act(k, l):
        return pltpu.make_async_remote_copy(
            src_ref=act_wire.at[k, l],
            dst_ref=act_wire.at[k, l],
            send_sem=act_sem.at[0, k, l],
            recv_sem=act_sem.at[1, k, l],
            device_id=(me_layer, me_feat, outer),
            device_id_type=MESH,
        )

    def encode(k):
        gather_wait(1, k, CORES if k else 1)
        first = ((y + SHIFTS[k]) % SIDE) * CORES
        for l in range(layers):
            if k == 0:
                load_enc[l].wait()
            some = rows[pl.ds(first, CORES), l].reshape(chunk_rows, -1)
            partial = jnp.dot(some, ew[l], preferred_element_type=F32)

            @pl.when(is_end)
            def _(l=l, partial=partial):
                outgoing[k, l] = to_wire(partial)
                send_part(k, l).start()

            @pl.when(is_mid)
            def _(l=l, partial=partial):
                part[k, l] = partial

    def pass_on(k):
        @pl.when(is_mid)
        def _():
            for l in range(layers):
                wait_part(0, k, l)
                summed = part[k, l] + from_wire(heard[0, k, l])
                outgoing[k, l] = to_wire(summed)
                send_part(k, l).start()
                part[k, l] = summed

    def finish(k):
        for l in range(layers):

            @pl.when(is_mid)
            def _(l=l):
                wait_part(1, k, l)
                pre = part[k, l] + from_wire(heard[1, k, l]) + eb[l : l + 1, :]
                pre = jnp.maximum(pre, 0.0)
                act_wire[k, l] = to_wire(pre)
                send_act(k, l).start()
                act[l] = pre

            @pl.when(is_end)
            def _(l=l):
                some = act_wire.at[k, l]
                pltpu.make_async_copy(some, some, act_sem.at[1, k, l]).wait()
                act[l] = from_wire(act_wire[k, l])

            decode(k, l)

    def decode(k, l):
        whole = act[l]
        high = whole.astype(BF16)
        low = (whole - high.astype(F32)).astype(BF16)
        both = jnp.concatenate([high, low], axis=0)
        for m in range(l, layers):
            b = block_of(m, l)
            twice = jnp.dot(both, dw_hi[b], preferred_element_type=F32)
            term = twice[:chunk_rows] + twice[chunk_rows:]
            term += jnp.dot(high, dw_lo[b], preferred_element_type=F32)
            term = term.reshape(CORES, own_rows, -1)
            if l == 0:
                total[k, m] = term
            else:
                total[k, m] += term

    def send_core(k):
        return pltpu.make_async_remote_copy(
            src_ref=total.at[k, :, 1 - core],
            dst_ref=core_in.at[k],
            send_sem=core_sem.at[0, k],
            recv_sem=core_sem.at[1, k],
            device_id=(y * CORES + 1 - core, me_feat, me_width),
            device_id_type=MESH,
        )

    own_plane = pltpu.make_async_copy(pair.at[0, x], plane_in.at[y * SIDE + x], own_sem.at[0])

    def send_plane(k, to_x):
        return pltpu.make_async_remote_copy(
            src_ref=pair.at[k, to_x],
            dst_ref=plane_in.at[y * SIDE + x],
            send_sem=plane_sem.at[0],
            recv_sem=plane_sem.at[1],
            device_id=(((y + SHIFTS[k]) % SIDE) * CORES + core, deep * SIDE + to_x, me_width),
            device_id_type=MESH,
        )

    def plane_wait(way):
        some = plane_in.at[pl.ds(0, SIDE * SIDE - 1)]
        pltpu.make_async_copy(some, some, plane_sem.at[way]).wait()

    def start_plane(k):
        send_core(k).wait_recv()
        if k == 0:
            pl.semaphore_wait(know_sem.at[4], SIDE - 1)
        both = total[k, :, core] + core_in[k]
        for to_x in range(SIDE):
            pair[k, to_x] = both[:, to_x * SIDE : (to_x + 1) * SIDE, :]
        if k == 0:
            own_plane.start()
        for d in (2, 1, 3, 0):
            if k or d:
                send_plane(k, (x + d) % SIDE).start()

    def send_ring(e):
        to_deep, to_width = (deep + e // SIDE) % SIDE, (me_width + e % SIDE) % SIDE
        return pltpu.make_async_remote_copy(
            src_ref=plane.at[to_deep],
            dst_ref=deep_in.at[deep * SIDE + me_width],
            send_sem=deep_sem.at[0],
            recv_sem=deep_sem.at[1],
            device_id=(me_layer, to_deep * SIDE + x, to_width),
            device_id_type=MESH,
        )

    def ring_wait(way):
        some = deep_in.at[pl.ds(0, SIDE * SIDE - 1)]
        pltpu.make_async_copy(some, some, deep_sem.at[way]).wait()

    def send_side(d):
        return pltpu.make_async_remote_copy(
            src_ref=side.at[me_width],
            dst_ref=side.at[me_width],
            send_sem=side_sem.at[0, d],
            recv_sem=side_sem.at[1, d],
            device_id=(me_layer, me_feat, (me_width + d) % SIDE),
            device_id_type=MESH,
        )

    encode(0)
    for b in range(blocks):
        split(b)
    load_bias.wait()
    load_db.wait()
    load_tg.wait()
    pass_on(0)
    encode(1)
    encode(2)
    encode(3)
    for l in range(layers):
        side[me_width, l : l + 1, :] = tg[l]
    side[me_width, layers : 2 * layers, :] = db[...]
    for d in range(1, SIDE):
        send_side(d).start()
    know_lines(0)
    pass_on(1)
    finish(0)
    send_core(0).start()
    pass_on(2)
    pass_on(3)
    know_lines(1)
    finish(1)
    send_core(1).start()
    start_plane(0)
    finish(2)
    send_core(2).start()
    start_plane(1)
    know_lines(2)
    finish(3)
    send_core(3).start()
    start_plane(2)
    for d in range(1, SIDE):
        send_side(d).wait_recv()

    @pl.when(is_mid)
    def _():
        pl.semaphore_wait(know_sem.at[3], 1)

    start_plane(3)
    own_plane.wait()
    plane_wait(1)
    summed = jnp.sum(plane_in[...], axis=0)
    for to in range(SIDE):
        for m in range(layers):
            plane[to, m : m + 1, :] = summed[m, to : to + 1, :]
    for e in (8, 9, 10, 11, 4, 12, 5, 6, 7, 13, 14, 15, 1, 2, 3):
        send_ring(e).start()
    deep_in[deep * SIDE + me_width] = plane[deep]
    ring_wait(1)

    sq_error = jnp.zeros((layers, 1), F32)
    sq_target = jnp.zeros((layers, 1), F32)
    for w in range(SIDE):
        whole = deep_in[w]
        for s in range(1, SIDE):
            whole = whole + deep_in[s * SIDE + w]
        wanted = side[w, 0:layers, :]
        diff = whole + side[w, layers : 2 * layers, :] - wanted
        sq_error += jnp.sum(diff * diff, axis=1, keepdims=True)
        sq_target += jnp.sum(wanted * wanted, axis=1, keepdims=True)
    err[...] = sq_error / (sq_target + 1e-06)
    whole = deep_in[me_width]
    for s in range(1, SIDE):
        whole = whole + deep_in[s * SIDE + me_width]
    whole = whole + db[...]
    for m in range(layers):
        recon[m] = whole[m : m + 1]

    gather_wait(0, 0, group - 1)
    plane_wait(0)
    ring_wait(0)
    for d in range(1, SIDE):
        send_side(d).wait_send()
    for k in range(SIDE):
        send_core(k).wait_send()
        for l in range(layers):
            send_part(k, l).wait_send()

            @pl.when(is_mid)
            def _(k=k, l=l):
                send_act(k, l).wait_send()


def per_device(resid, enc_w, enc_b, dec_w, dec_b, target):
    layers, own_rows, wide = resid.shape
    features = enc_w.shape[2]
    blocks, _, width = dec_w.shape
    group = SIDE * CORES
    chunk_rows = CORES * own_rows
    vm = pltpu.VMEM
    dma = pltpu.SemaphoreType.DMA
    in_hbm = pl.BlockSpec(memory_space=pltpu.HBM)
    in_vmem = pl.BlockSpec(memory_space=pltpu.VMEM)
    return pl.pallas_call(
        functools.partial(kernel, layers),
        out_shape=(
            jax.ShapeDtypeStruct((layers, 1, width), F32),
            jax.ShapeDtypeStruct((layers, 1), F32),
        ),
        in_specs=[in_hbm] * 6,
        out_specs=(in_vmem, in_vmem),
        scratch_shapes=[
            vm((layers, own_rows, wide), BF16),
            vm((group, layers, own_rows, wide), BF16),
            vm((layers, wide, features), BF16),
            vm((layers, features), F32),
            vm((blocks, features, width), F32),
            vm((blocks, features, width), BF16),
            vm((blocks, features, width), BF16),
            vm((layers, width), F32),
            vm((layers, 1, width), F32),
            vm((SIDE, layers, chunk_rows, features), F32),
            vm((SIDE, layers, chunk_rows, features), WIRE),
            vm((2, SIDE, layers, chunk_rows, features), WIRE),
            vm((SIDE, layers, chunk_rows, features), WIRE),
            vm((layers, chunk_rows, features), F32),
            vm((SIDE, layers, CORES, own_rows, width), F32),
            vm((SIDE, layers, own_rows, width), F32),
            vm((SIDE, SIDE, layers, SIDE, width), F32),
            vm((SIDE * SIDE, layers, SIDE, width), F32),
            vm((SIDE, layers, width), F32),
            vm((SIDE * SIDE, layers, width), F32),
            vm((SIDE, 2 * layers, width), F32),
            dma((4,)),
            dma((layers,)),
            dma((blocks,)),
            dma((2, SIDE)),
            dma((3, SIDE, layers)),
            dma((2, SIDE, layers)),
            dma((2, SIDE)),
            dma((2,)),
            dma((1,)),
            dma((2,)),
            dma((2, SIDE)),
            pltpu.SemaphoreType.REGULAR((5,)),
        ],
        compiler_params=pltpu.CompilerParams(
            collective_id=0, has_side_effects=True, vmem_limit_bytes=56 * 1024 * 1024
        ),
        cost_estimate=pl.CostEstimate(
            flops=1_400_000_000, bytes_accessed=4_500_000, transcendentals=1_500_000
        ),
    )(resid, enc_w, enc_b, dec_w, dec_b, target)


def solution(mesh):
    in_specs = (
        P(None, "layer", "width"),
        P(None, "width", ("layer", "feat")),
        P(None, ("layer", "feat")),
        P(None, ("layer", "feat"), "width"),
        P(None, "width"),
        P(None, ("layer", "feat"), "width"),
    )
    out_specs = (P(None, ("layer", "feat"), "width"), P(None, ("layer", "feat")))
    return jax.shard_map(
        per_device, mesh=mesh, in_specs=in_specs, out_specs=out_specs, check_vma=False
    )
```

time: 1590 us -> 49 us (0.03); the launches traced: 1570 us -> 48.8 us
  waiting for transfers between devices: 1510 us -> 0 us
  Pallas kernels: 0 us -> 45.7 us
  blocking collectives: 27.8 us -> 0 us
    unnamed x3 -> x0, waiting for transfers between devices: 1450 us -> none
    psum x1 -> x0, waiting for transfers between devices: 58.7 us -> none  [per_device(): pre = lax.psum(partial_pre, 'width')]
    pallas_call x0 -> x1, Pallas kernels: none -> 45.7 us  [per_device(): pl.pallas_call(functools.partial(kernel, layers), out_shape=(jax.ShapeDty...]
    all_gather x1 -> x0, blocking collectives: 19.9 us -> none  [per_device(): gathered = lax.all_gather(resid, 'layer', axis=1, tiled=True)]
  transfers between devices with their start and end apart: 2 -> 0, of which waited for: 2 -> 0; matrix products, arithmetic and copies ran while one was open for 0% -> 0% of each run, Pallas kernels for 0% -> 0%
where the time goes in v2:
time: 49 us; the launch traced here: 48.8 us
  Pallas kernels  45.7 us (93%)
  local copies, waits for them, and re-layouts  2.51 us (5%)
  between operations  0.64 us (1%)
    pallas_call x1, Pallas kernels, per_device(): pl.pallas_call(functools.partial(kernel, layers), out_shape=(jax.ShapeDty...  45.7 us
    unnamed x1, local copies, waits for them, and re-layouts  1.26 us
    pallas_call x1, local copies, waits for them, and re-layouts, per_device(): pl.pallas_call(functools.partial(kernel, layers), out_shape=(jax.ShapeDty...  1.24 us

profile of v2, /device:TPU:1, one launch (start us, length us, event | category | flops | bytes accessed | tf_op | source)
XLA Modules:
  0.0 48.8 jit_solution(16784784643948372249)
XLA Ops:
  0.6 45.7 %shard_map.77 = (f32[2,1,512]{2,1,0:T(1,128)}, f32[2,1]{1,0:T(2,128)}) custom-call(bf16[2,16,512]{2,1,0:T(8,128)(2,1)} %resid.1, bf16[2,512,512]{2,1,0:T(8,128)(2,1)} %enc_w.1, f32[2,512]{1,0:T(2,128)} %enc_b.1, f32[3,512,512]{2,1,0:T(8,128)} %dec_w.1, f32[2,512]{1,0:T(2,128)} %dec_b.1, f32[2,1,512]{2,1,0:T(1,128)} %target.1), custom_call_target="tpu_custom_call" | custom-call | flops 1400000000 | bytes 4500000 | tf_op jit(solution)/shard_map/pallas_call | solution.py:445
  46.3 1.2 %copy.8 = f32[2,1]{0,1:T(1,128)} copy(f32[2,1]{1,0:T(2,128)} %get-tuple-element.3) | data formatting | bytes 16 | tf_op jit(solution)/shard_map/pallas_call | solution.py:445
  47.6 1.3 %copy.10 = f32[2,1,512]{2,1,0:T(1,128)} copy(f32[2,1,512]{2,1,0:T(1,128)} %get-tuple-element.6) | data formatting | bytes 8192

commit v3 on v2

--- a/solution.py
+++ b/solution.py
@@ -12,7 +12,7 @@
 BF16 = jnp.bfloat16
 CORES = 2
 SIDE = 4
-SHIFTS = (0, 1, 3, 2)
+ORDER = ((0, 0), (0, 1), (1, 0), (3, 0), (2, 0), (2, 1), (1, 1), (3, 1))
 
 WIRE = BF16
 POWER = 12.0
@@ -44,7 +44,6 @@
     dec_b,
     target,
     recon,
-    err,
     own_in,
     rows,
     ew,
@@ -104,19 +103,16 @@
 
     barrier = pltpu.get_barrier_semaphore()
 
-    def greet_layer(d, carry):
-        signal(barrier, (me_layer + d) % group, me_feat, me_width)
-        return carry
-
-    def greet_others(d, carry):
-        signal(barrier, me_layer, me_feat, (me_width + d) % SIDE)
-        signal(barrier, me_layer, deep * SIDE + (x + d) % SIDE, me_width)
-        return carry
-
     load_rows = pltpu.make_async_copy(resid, own_in, in_sem.at[0])
     load_rows.start()
-    lax.fori_loop(1, group, greet_layer, 0)
-    lax.fori_loop(1, SIDE, greet_others, 0)
+    for d in (4, 3, 5, 2, 6):
+        signal(barrier, (me_layer + d) % group, me_feat, me_width)
+    for d in range(1, SIDE):
+        signal(barrier, me_layer, me_feat, (me_width + d) % SIDE)
+    for d in range(1, SIDE):
+        signal(barrier, me_layer, deep * SIDE + (x + d) % SIDE, me_width)
+    for d in (1, 7):
+        signal(barrier, (me_layer + d) % group, me_feat, me_width)
 
     @pl.when(is_end)
     def _():
@@ -141,25 +137,28 @@
     near = group - 1 + 2 * (SIDE - 1)
     pl.semaphore_wait(barrier, jnp.where(is_end, near + 1, near))
 
-    def push(k, to_core):
-        to = ((y + SHIFTS[k]) % SIDE) * CORES + to_core
+    def push(k, l, to_core):
         pltpu.make_async_remote_copy(
-            src_ref=rows.at[me_layer],
-            dst_ref=rows.at[me_layer],
-            send_sem=gather_sem.at[0, 0],
-            recv_sem=gather_sem.at[1, SHIFTS.index((SIDE - SHIFTS[k]) % SIDE)],
-            device_id=(to, me_feat, me_width),
+            src_ref=rows.at[me_layer, l],
+            dst_ref=rows.at[me_layer, l],
+            send_sem=gather_sem.at[0, 0, 0],
+            recv_sem=gather_sem.at[1, (SIDE - k) % SIDE, l],
+            device_id=(((y + k) % SIDE) * CORES + to_core, me_feat, me_width),
             device_id_type=MESH,
         ).start()
 
-    push(0, 1 - core)
-    for k in (3, 1, 2):
-        push(k, core)
-        push(k, 1 - core)
-
-    def gather_wait(way, k, count):
-        some = rows.at[pl.ds(0, count)]
-        pltpu.make_async_copy(some, some, gather_sem.at[way, k]).wait()
+    for k, l in ORDER:
+        if k:
+            push(k, l, core)
+        push(k, l, 1 - core)
+
+    def gather_wait(k, l):
+        some = rows.at[pl.ds(0, CORES if k else 1), l]
+        pltpu.make_async_copy(some, some, gather_sem.at[1, k, l]).wait()
+
+    def gather_sent():
+        some = rows.at[pl.ds(0, group - 1)]
+        pltpu.make_async_copy(some, some, gather_sem.at[0, 0, 0]).wait()
 
     def greet_row(d, carry):
         signal(know_sem.at[4], me_layer, deep * SIDE + (x + d) % SIDE, me_width)
@@ -220,56 +219,53 @@
             device_id_type=MESH,
         )
 
-    def encode(k):
-        gather_wait(1, k, CORES if k else 1)
-        first = ((y + SHIFTS[k]) % SIDE) * CORES
-        for l in range(layers):
-            if k == 0:
-                load_enc[l].wait()
-            some = rows[pl.ds(first, CORES), l].reshape(chunk_rows, -1)
-            partial = jnp.dot(some, ew[l], preferred_element_type=F32)
-
-            @pl.when(is_end)
-            def _(l=l, partial=partial):
-                outgoing[k, l] = to_wire(partial)
-                send_part(k, l).start()
-
-            @pl.when(is_mid)
-            def _(l=l, partial=partial):
-                part[k, l] = partial
-
-    def pass_on(k):
+    def encode(k, l):
+        gather_wait(k, l)
+        if k == 0:
+            load_enc[l].wait()
+        first = ((y + k) % SIDE) * CORES
+        some = rows[pl.ds(first, CORES), l].reshape(chunk_rows, -1)
+        partial = jnp.dot(some, ew[l], preferred_element_type=F32)
+
+        @pl.when(is_end)
+        def _():
+            outgoing[k, l] = to_wire(partial)
+            send_part(k, l).start()
+
         @pl.when(is_mid)
         def _():
-            for l in range(layers):
-                wait_part(0, k, l)
-                summed = part[k, l] + from_wire(heard[0, k, l])
-                outgoing[k, l] = to_wire(summed)
-                send_part(k, l).start()
-                part[k, l] = summed
-
-    def finish(k):
-        for l in range(layers):
-
-            @pl.when(is_mid)
-            def _(l=l):
-                wait_part(1, k, l)
-                pre = part[k, l] + from_wire(heard[1, k, l]) + eb[l : l + 1, :]
-                pre = jnp.maximum(pre, 0.0)
-                act_wire[k, l] = to_wire(pre)
-                send_act(k, l).start()
-                act[l] = pre
-
-            @pl.when(is_end)
-            def _(l=l):
-                some = act_wire.at[k, l]
-                pltpu.make_async_copy(some, some, act_sem.at[1, k, l]).wait()
-                act[l] = from_wire(act_wire[k, l])
-
-            decode(k, l)
+            part[k, l] = partial
+
+    def pass_on(k, l):
+        @pl.when(is_mid)
+        def _():
+            wait_part(0, k, l)
+            summed = part[k, l] + from_wire(heard[0, k, l])
+            outgoing[k, l] = to_wire(summed)
+            send_part(k, l).start()
+            part[k, l] = summed
+
+    def finish(k, l):
+        @pl.when(is_mid)
+        def _():
+            wait_part(1, k, l)
+            pre = part[k, l] + from_wire(heard[1, k, l]) + eb[l : l + 1, :]
+            pre = jnp.maximum(pre, 0.0)
+            act_wire[k, l] = to_wire(pre)
+            send_act(k, l).start()
+            act[...] = pre
+
+        @pl.when(is_end)
+        def _():
+            some = act_wire.at[k, l]
+            pltpu.make_async_copy(some, some, act_sem.at[1, k, l]).wait()
+            act[...] = from_wire(act_wire[k, l])
+
+        decode(k, l)
+        send_core(k, l).start()
 
     def decode(k, l):
-        whole = act[l]
+        whole = act[...]
         high = whole.astype(BF16)
         low = (whole - high.astype(F32)).astype(BF16)
         both = jnp.concatenate([high, low], axis=0)
@@ -284,44 +280,42 @@
             else:
                 total[k, m] += term
 
-    def send_core(k):
+    def send_core(k, m):
         return pltpu.make_async_remote_copy(
-            src_ref=total.at[k, :, 1 - core],
-            dst_ref=core_in.at[k],
-            send_sem=core_sem.at[0, k],
-            recv_sem=core_sem.at[1, k],
+            src_ref=total.at[k, m, 1 - core],
+            dst_ref=core_in.at[k, m],
+            send_sem=core_sem.at[0, k, m],
+            recv_sem=core_sem.at[1, k, m],
             device_id=(y * CORES + 1 - core, me_feat, me_width),
             device_id_type=MESH,
         )
 
     own_plane = pltpu.make_async_copy(pair.at[0, x], plane_in.at[y * SIDE + x], own_sem.at[0])
 
-    def send_plane(k, to_x):
-        return pltpu.make_async_remote_copy(
-            src_ref=pair.at[k, to_x],
-            dst_ref=plane_in.at[y * SIDE + x],
-            send_sem=plane_sem.at[0],
-            recv_sem=plane_sem.at[1],
-            device_id=(((y + SHIFTS[k]) % SIDE) * CORES + core, deep * SIDE + to_x, me_width),
-            device_id_type=MESH,
-        )
+    def start_plane(k, m):
+        send_core(k, m).wait_recv()
+        if (k, m) == ORDER[0]:
+            pl.semaphore_wait(know_sem.at[4], SIDE - 1)
+        both = total[k, m, core] + core_in[k, m]
+        for to_x in range(SIDE):
+            pair[k, to_x, m] = both[to_x * SIDE : (to_x + 1) * SIDE, :]
+        if (k, m) == (0, layers - 1):
+            own_plane.start()
+        for d in (2, 1, 3, 0):
+            if k or d:
+                to_x = (x + d) % SIDE
+                pltpu.make_async_remote_copy(
+                    src_ref=pair.at[k, to_x, m],
+                    dst_ref=plane_in.at[y * SIDE + x, m],
+                    send_sem=plane_sem.at[0],
+                    recv_sem=plane_sem.at[1],
+                    device_id=(((y + k) % SIDE) * CORES + core, deep * SIDE + to_x, me_width),
+                    device_id_type=MESH,
+                ).start()
 
     def plane_wait(way):
         some = plane_in.at[pl.ds(0, SIDE * SIDE - 1)]
         pltpu.make_async_copy(some, some, plane_sem.at[way]).wait()
-
-    def start_plane(k):
-        send_core(k).wait_recv()
-        if k == 0:
-            pl.semaphore_wait(know_sem.at[4], SIDE - 1)
-        both = total[k, :, core] + core_in[k]
-        for to_x in range(SIDE):
-            pair[k, to_x] = both[:, to_x * SIDE : (to_x + 1) * SIDE, :]
-        if k == 0:
-            own_plane.start()
-        for d in (2, 1, 3, 0):
-            if k or d:
-                send_plane(k, (x + d) % SIDE).start()
 
     def send_ring(e):
         to_deep, to_width = (deep + e // SIDE) % SIDE, (me_width + e % SIDE) % SIDE
@@ -348,46 +342,52 @@
             device_id_type=MESH,
         )
 
-    encode(0)
-    for b in range(blocks):
-        split(b)
-    load_bias.wait()
-    load_db.wait()
-    load_tg.wait()
-    pass_on(0)
-    encode(1)
-    encode(2)
-    encode(3)
-    for l in range(layers):
-        side[me_width, l : l + 1, :] = tg[l]
-    side[me_width, layers : 2 * layers, :] = db[...]
-    for d in range(1, SIDE):
-        send_side(d).start()
-    know_lines(0)
-    pass_on(1)
-    finish(0)
-    send_core(0).start()
-    pass_on(2)
-    pass_on(3)
-    know_lines(1)
-    finish(1)
-    send_core(1).start()
-    start_plane(0)
-    finish(2)
-    send_core(2).start()
-    start_plane(1)
-    know_lines(2)
-    finish(3)
-    send_core(3).start()
-    start_plane(2)
+    def share_side():
+        load_db.wait()
+        load_tg.wait()
+        for l in range(layers):
+            side[me_width, l : l + 1, :] = tg[l]
+        side[me_width, layers : 2 * layers, :] = db[...]
+        for d in range(1, SIDE):
+            send_side(d).start()
+
+    def ready():
+        for b in range(blocks):
+            split(b)
+        load_bias.wait()
+
+    steps = dict(e=encode, p=pass_on, f=finish, c=start_plane)
+    plan = (
+        "e0 e1 R e2",
+        "e3 p0 e4 p1",
+        "e5 e6 e7 S",
+        "k0 p2 p3 f0",
+        "p4 p5 f1 k1",
+        "p6 f2 c0 p7",
+        "f3 c1 k2 f4",
+        "c2 f5 c3 f6",
+        "c4 f7 c5 c6",
+    )
+    for word in " ".join(plan).split():
+        if word == "R":
+            ready()
+        elif word == "S":
+            share_side()
+        elif word[0] == "k":
+            know_lines(int(word[1]))
+        else:
+            steps[word[0]](*ORDER[int(word[1])])
     for d in range(1, SIDE):
         send_side(d).wait_recv()
+    wanted = [side[w, 0:layers, :] for w in range(SIDE)]
+    sq_target = jnp.sum(sum(v * v for v in wanted), axis=1, keepdims=True)
+    away = [side[w, layers : 2 * layers, :] - wanted[w] for w in range(SIDE)]
 
     @pl.when(is_mid)
     def _():
         pl.semaphore_wait(know_sem.at[3], 1)
 
-    start_plane(3)
+    start_plane(*ORDER[-1])
     own_plane.wait()
     plane_wait(1)
     summed = jnp.sum(plane_in[...], axis=0)
@@ -399,37 +399,44 @@
     deep_in[deep * SIDE + me_width] = plane[deep]
     ring_wait(1)
 
-    sq_error = jnp.zeros((layers, 1), F32)
-    sq_target = jnp.zeros((layers, 1), F32)
+    squares = jnp.zeros((layers, deep_in.shape[2]), F32)
     for w in range(SIDE):
         whole = deep_in[w]
         for s in range(1, SIDE):
             whole = whole + deep_in[s * SIDE + w]
-        wanted = side[w, 0:layers, :]
-        diff = whole + side[w, layers : 2 * layers, :] - wanted
-        sq_error += jnp.sum(diff * diff, axis=1, keepdims=True)
-        sq_target += jnp.sum(wanted * wanted, axis=1, keepdims=True)
-    err[...] = sq_error / (sq_target + 1e-06)
+        diff = whole + away[w]
+        squares += diff * diff
+    sq_error = jnp.sum(squares, axis=1, keepdims=True)
+    ratio = sq_error / (sq_target + 1e-06)
+    lane = lax.broadcasted_iota(jnp.int32, (1, whole.shape[1]), 1)
+    row = jnp.broadcast_to(ratio[0:1], lane.shape)
+    for m in range(1, layers):
+        row = jnp.where(lane == m, ratio[m : m + 1], row)
+    recon[layers : layers + 1, :] = row
     whole = deep_in[me_width]
     for s in range(1, SIDE):
         whole = whole + deep_in[s * SIDE + me_width]
     whole = whole + db[...]
-    for m in range(layers):
-        recon[m] = whole[m : m + 1]
-
-    gather_wait(0, 0, group - 1)
+    recon[0:layers, :] = whole
+
+    gather_sent()
     plane_wait(0)
     ring_wait(0)
     for d in range(1, SIDE):
         send_side(d).wait_send()
-    for k in range(SIDE):
-        send_core(k).wait_send()
-        for l in range(layers):
-            send_part(k, l).wait_send()
-
-            @pl.when(is_mid)
-            def _(k=k, l=l):
-                send_act(k, l).wait_send()
+    for k, l in ORDER:
+        send_core(k, l).wait_send()
+        send_part(k, l).wait_send()
+
+        @pl.when(is_mid)
+        def _(k=k, l=l):
+            send_act(k, l).wait_send()
+
+
+def divide(layers, both, recon, err):
+    for m in range(layers):
+        recon[m] = both[m : m + 1, :]
+    err[...] = both[layers : layers + 1, 0:layers]
 
 
 def per_device(resid, enc_w, enc_b, dec_w, dec_b, target):
@@ -442,14 +449,11 @@
     dma = pltpu.SemaphoreType.DMA
     in_hbm = pl.BlockSpec(memory_space=pltpu.HBM)
     in_vmem = pl.BlockSpec(memory_space=pltpu.VMEM)
-    return pl.pallas_call(
+    both = pl.pallas_call(
         functools.partial(kernel, layers),
-        out_shape=(
-            jax.ShapeDtypeStruct((layers, 1, width), F32),
-            jax.ShapeDtypeStruct((layers, 1), F32),
-        ),
+        out_shape=pltpu.VMEM((layers + 1, width), F32),
         in_specs=[in_hbm] * 6,
-        out_specs=(in_vmem, in_vmem),
+        out_specs=in_vmem,
         scratch_shapes=[
             vm((layers, own_rows, wide), BF16),
             vm((group, layers, own_rows, wide), BF16),
@@ -464,7 +468,7 @@
             vm((SIDE, layers, chunk_rows, features), WIRE),
             vm((2, SIDE, layers, chunk_rows, features), WIRE),
             vm((SIDE, layers, chunk_rows, features), WIRE),
-            vm((layers, chunk_rows, features), F32),
+            vm((chunk_rows, features), F32),
             vm((SIDE, layers, CORES, own_rows, width), F32),
             vm((SIDE, layers, own_rows, width), F32),
             vm((SIDE, SIDE, layers, SIDE, width), F32),
@@ -475,10 +479,10 @@
             dma((4,)),
             dma((layers,)),
             dma((blocks,)),
-            dma((2, SIDE)),
+            dma((2, SIDE, layers)),
             dma((3, SIDE, layers)),
             dma((2, SIDE, layers)),
-            dma((2, SIDE)),
+            dma((2, SIDE, layers)),
             dma((2,)),
             dma((1,)),
             dma((2,)),
@@ -492,6 +496,17 @@
             flops=1_400_000_000, bytes_accessed=4_500_000, transcendentals=1_500_000
         ),
     )(resid, enc_w, enc_b, dec_w, dec_b, target)
+    recon, err = pl.pallas_call(
+        functools.partial(divide, layers),
+        out_shape=(
+            jax.ShapeDtypeStruct((layers, 1, width), F32),
+            jax.ShapeDtypeStruct((1, layers), F32),
+        ),
+        in_specs=[in_vmem],
+        out_specs=(in_vmem, in_vmem),
+        compiler_params=pltpu.CompilerParams(vmem_limit_bytes=1024 * 1024),
+    )(both)
+    return recon, err.reshape(layers, 1)
 
 
 def solution(mesh):

time: 49 us -> 45.1 us (0.920)
  local copies, waits for them, and re-layouts: 2.51 us -> 0 us
  Pallas kernels: 45.7 us -> 44.4 us
    pallas_call x1 -> x2, Pallas kernels: 45.7 us -> 44.4 us  [the longest x1 43.8 us: per_device(): pl.pallas_call(functools.partial(kernel, layers), out_shape=pltpu.VMEM((l...]
    unnamed x1 -> x0, local copies, waits for them, and re-layouts: 1.26 us -> none
    pallas_call x1 -> x0, local copies, waits for them, and re-layouts: 1.24 us -> none  [per_device(): pl.pallas_call(functools.partial(kernel, layers), out_shape=(jax.ShapeDty...]
where the time goes in v3:
time: 45.1 us; the launch traced here: 45 us
  Pallas kernels  44.4 us (98%)
  between operations  0.64 us (1%)
    pallas_call x1, Pallas kernels, per_device(): pl.pallas_call(functools.partial(kernel, layers), out_shape=pltpu.VMEM((l...  43.8 us

profile of v3, /device:TPU:1, one launch (start us, length us, event | category | flops | bytes accessed | tf_op | source)
XLA Modules:
  0.0 45.0 jit_solution(12101514966469416909)
XLA Ops:
  0.6 43.8 %shard_map.77.both = f32[3,512]{1,0:T(4,128)S(1)} custom-call(bf16[2,16,512]{2,1,0:T(8,128)(2,1)} %resid.1, bf16[2,512,512]{2,1,0:T(8,128)(2,1)} %enc_w.1, f32[2,512]{1,0:T(2,128)} %enc_b.1, f32[3,512,512]{2,1,0:T(8,128)} %dec_w.1, f32[2,512]{1,0:T(2,128)} %dec_b.1, f32[2,1,512]{2,1,0:T(1,128)} %target.1), custom_call_target="tpu_custom_call" | custom-call | flops 1400000000 | bytes 4500000 | tf_op jit(solution)/shard_map/pallas_call | solution.py:452
  44.4 0.6 %shard_map.78 = (f32[2,1,512]{2,1,0:T(1,128)}, f32[1,2]{1,0:T(1,128)}) custom-call(f32[3,512]{1,0:T(4,128)S(1)} %shard_map.77.both), custom_call_target="tpu_custom_call" | custom-call | tf_op jit(solution)/shard_map/pallas_call | solution.py:499

commit v4 on v3

--- a/solution.py
+++ b/solution.py
@@ -59,7 +59,6 @@
     act_wire,
     act,
     total,
-    core_in,
     pair,
     plane_in,
     plane,
@@ -71,7 +70,6 @@
     gather_sem,
     part_sem,
     act_sem,
-    core_sem,
     plane_sem,
     own_sem,
     deep_sem,
@@ -262,7 +260,6 @@
             act[...] = from_wire(act_wire[k, l])
 
         decode(k, l)
-        send_core(k, l).start()
 
     def decode(k, l):
         whole = act[...]
@@ -274,47 +271,44 @@
             twice = jnp.dot(both, dw_hi[b], preferred_element_type=F32)
             term = twice[:chunk_rows] + twice[chunk_rows:]
             term += jnp.dot(high, dw_lo[b], preferred_element_type=F32)
-            term = term.reshape(CORES, own_rows, -1)
-            if l == 0:
+            if l > 0:
+                term += total[k, m]
+            if m == l:
+                start_plane(k, m, term)
+            else:
                 total[k, m] = term
-            else:
-                total[k, m] += term
-
-    def send_core(k, m):
-        return pltpu.make_async_remote_copy(
-            src_ref=total.at[k, m, 1 - core],
-            dst_ref=core_in.at[k, m],
-            send_sem=core_sem.at[0, k, m],
-            recv_sem=core_sem.at[1, k, m],
-            device_id=(y * CORES + 1 - core, me_feat, me_width),
-            device_id_type=MESH,
-        )
-
-    own_plane = pltpu.make_async_copy(pair.at[0, x], plane_in.at[y * SIDE + x], own_sem.at[0])
-
-    def start_plane(k, m):
-        send_core(k, m).wait_recv()
+
+    mine = me_layer * SIDE + x
+    own_plane = [
+        pltpu.make_async_copy(pair.at[0, m, core, x], plane_in.at[mine, m], own_sem.at[m])
+        for m in range(layers)
+    ]
+
+    def start_plane(k, m, summed):
         if (k, m) == ORDER[0]:
             pl.semaphore_wait(know_sem.at[4], SIDE - 1)
-        both = total[k, m, core] + core_in[k, m]
-        for to_x in range(SIDE):
-            pair[k, to_x, m] = both[to_x * SIDE : (to_x + 1) * SIDE, :]
-        if (k, m) == (0, layers - 1):
-            own_plane.start()
+        for to_core in range(CORES):
+            for to_x in range(SIDE):
+                first = to_core * own_rows + to_x * SIDE
+                pair[k, m, to_core, to_x] = summed[first : first + SIDE, :]
+        if k == 0:
+            own_plane[m].start()
         for d in (2, 1, 3, 0):
-            if k or d:
-                to_x = (x + d) % SIDE
-                pltpu.make_async_remote_copy(
-                    src_ref=pair.at[k, to_x, m],
-                    dst_ref=plane_in.at[y * SIDE + x, m],
-                    send_sem=plane_sem.at[0],
-                    recv_sem=plane_sem.at[1],
-                    device_id=(((y + k) % SIDE) * CORES + core, deep * SIDE + to_x, me_width),
-                    device_id_type=MESH,
-                ).start()
+            for e in range(CORES):
+                if k or d or e:
+                    to_x, to_core = (x + d) % SIDE, (core + e) % CORES
+                    to_layer = ((y + k) % SIDE) * CORES + to_core
+                    pltpu.make_async_remote_copy(
+                        src_ref=pair.at[k, m, to_core, to_x],
+                        dst_ref=plane_in.at[mine, m],
+                        send_sem=plane_sem.at[0],
+                        recv_sem=plane_sem.at[1],
+                        device_id=(to_layer, deep * SIDE + to_x, me_width),
+                        device_id_type=MESH,
+                    ).start()
 
     def plane_wait(way):
-        some = plane_in.at[pl.ds(0, SIDE * SIDE - 1)]
+        some = plane_in.at[pl.ds(0, group * SIDE - 1)]
         pltpu.make_async_copy(some, some, plane_sem.at[way]).wait()
 
     def send_ring(e):
@@ -356,17 +350,16 @@
             split(b)
         load_bias.wait()
 
-    steps = dict(e=encode, p=pass_on, f=finish, c=start_plane)
+    steps = dict(e=encode, p=pass_on, f=finish)
     plan = (
         "e0 e1 R e2",
         "e3 p0 e4 p1",
         "e5 e6 e7 S",
         "k0 p2 p3 f0",
         "p4 p5 f1 k1",
-        "p6 f2 c0 p7",
-        "f3 c1 k2 f4",
-        "c2 f5 c3 f6",
-        "c4 f7 c5 c6",
+        "p6 f2 p7 f3",
+        "k2 f4 f5 f6",
+        "f7",
     )
     for word in " ".join(plan).split():
         if word == "R":
@@ -387,8 +380,8 @@
     def _():
         pl.semaphore_wait(know_sem.at[3], 1)
 
-    start_plane(*ORDER[-1])
-    own_plane.wait()
+    for m in range(layers):
+        own_plane[m].wait()
     plane_wait(1)
     summed = jnp.sum(plane_in[...], axis=0)
     for to in range(SIDE):
@@ -425,7 +418,6 @@
     for d in range(1, SIDE):
         send_side(d).wait_send()
     for k, l in ORDER:
-        send_core(k, l).wait_send()
         send_part(k, l).wait_send()
 
         @pl.when(is_mid)
@@ -469,10 +461,9 @@
             vm((2, SIDE, layers, chunk_rows, features), WIRE),
             vm((SIDE, layers, chunk_rows, features), WIRE),
             vm((chunk_rows, features), F32),
-            vm((SIDE, layers, CORES, own_rows, width), F32),
-            vm((SIDE, layers, own_rows, width), F32),
-            vm((SIDE, SIDE, layers, SIDE, width), F32),
-            vm((SIDE * SIDE, layers, SIDE, width), F32),
+            vm((SIDE, layers, chunk_rows, width), F32),
+            vm((SIDE, layers, CORES, SIDE, SIDE, width), F32),
+            vm((group * SIDE, layers, SIDE, width), F32),
             vm((SIDE, layers, width), F32),
             vm((SIDE * SIDE, layers, width), F32),
             vm((SIDE, 2 * layers, width), F32),
@@ -482,9 +473,8 @@
             dma((2, SIDE, layers)),
             dma((3, SIDE, layers)),
             dma((2, SIDE, layers)),
-            dma((2, SIDE, layers)),
             dma((2,)),
-            dma((1,)),
+            dma((layers,)),
             dma((2,)),
             dma((2, SIDE)),
             pltpu.SemaphoreType.REGULAR((5,)),

time: 45.1 us -> 44.7 us (level)
  Pallas kernels: 44.4 us -> 43.9 us
where the time goes in v4:
time: 44.7 us; the launch traced here: 44.6 us
  Pallas kernels  43.9 us (98%)
  between operations  0.64 us (1%)
    pallas_call x1, Pallas kernels, per_device(): pl.pallas_call(functools.partial(kernel, layers), out_shape=pltpu.VMEM((l...  43.3 us

profile of v4, /device:TPU:1, one launch (start us, length us, event | category | flops | bytes accessed | tf_op | source)
XLA Modules:
  0.0 44.6 jit_solution(5439829749544339083)
XLA Ops:
  0.6 43.3 %shard_map.77.both = f32[3,512]{1,0:T(4,128)S(1)} custom-call(bf16[2,16,512]{2,1,0:T(8,128)(2,1)} %resid.1, bf16[2,512,512]{2,1,0:T(8,128)(2,1)} %enc_w.1, f32[2,512]{1,0:T(2,128)} %enc_b.1, f32[3,512,512]{2,1,0:T(8,128)} %dec_w.1, f32[2,512]{1,0:T(2,128)} %dec_b.1, f32[2,1,512]{2,1,0:T(1,128)} %target.1), custom_call_target="tpu_custom_call" | custom-call | flops 1400000000 | bytes 4500000 | tf_op jit(solution)/shard_map/pallas_call | solution.py:444
  44.0 0.6 %shard_map.78 = (f32[2,1,512]{2,1,0:T(1,128)}, f32[1,2]{1,0:T(1,128)}) custom-call(f32[3,512]{1,0:T(4,128)S(1)} %shard_map.77.both), custom_call_target="tpu_custom_call" | custom-call | tf_op jit(solution)/shard_map/pallas_call | solution.py:489

commit v5 on v4

--- a/solution.py
+++ b/solution.py
@@ -12,7 +12,7 @@
 BF16 = jnp.bfloat16
 CORES = 2
 SIDE = 4
-ORDER = ((0, 0), (0, 1), (1, 0), (3, 0), (2, 0), (2, 1), (1, 1), (3, 1))
+ORDER = ((0, 0), (0, 1), (2, 0), (2, 1), (1, 0), (3, 0), (1, 1), (3, 1))
 
 WIRE = BF16
 POWER = 12.0

time: 44.7 us -> 44.3 us (level)
    pallas_call x1, Pallas kernels: 43.3 us -> 42.9 us  [per_device(): pl.pallas_call(functools.partial(kernel, layers), out_shape=pltpu.VMEM((l...]
where the time goes in v5:
time: 44.3 us; the launch traced here: 44.1 us
  Pallas kernels  43.5 us (98%)
  between operations  0.64 us (1%)
    pallas_call x1, Pallas kernels, per_device(): pl.pallas_call(functools.partial(kernel, layers), out_shape=pltpu.VMEM((l...  42.9 us

profile of v5, /device:TPU:1, one launch (start us, length us, event | category | flops | bytes accessed | tf_op | source)
XLA Modules:
  0.0 44.1 jit_solution(7453251271419647742)
XLA Ops:
  0.6 42.9 %shard_map.77.both = f32[3,512]{1,0:T(4,128)S(1)} custom-call(bf16[2,16,512]{2,1,0:T(8,128)(2,1)} %resid.1, bf16[2,512,512]{2,1,0:T(8,128)(2,1)} %enc_w.1, f32[2,512]{1,0:T(2,128)} %enc_b.1, f32[3,512,512]{2,1,0:T(8,128)} %dec_w.1, f32[2,512]{1,0:T(2,128)} %dec_b.1, f32[2,1,512]{2,1,0:T(1,128)} %target.1), custom_call_target="tpu_custom_call" | custom-call | flops 1400000000 | bytes 4500000 | tf_op jit(solution)/shard_map/pallas_call | solution.py:444
  43.5 0.6 %shard_map.78 = (f32[2,1,512]{2,1,0:T(1,128)}, f32[1,2]{1,0:T(1,128)}) custom-call(f32[3,512]{1,0:T(4,128)S(1)} %shard_map.77.both), custom_call_target="tpu_custom_call" | custom-call | tf_op jit(solution)/shard_map/pallas_call | solution.py:489

commit v6 on v5

--- a/solution.py
+++ b/solution.py
@@ -18,6 +18,9 @@
 POWER = 12.0
 BASE = 124.0
 FINE = 2.0**-10
+
+
+PIECES = 2
 
 
 def to_wire(value):
@@ -86,6 +89,7 @@
     features = ew.shape[2]
     blocks = dw.shape[0]
     chunk_rows = CORES * own_rows
+    wide = features // PIECES
 
     is_low = me_width == 0
     is_high = me_width == SIDE - 1
@@ -193,26 +197,26 @@
 
         lax.fori_loop(0, features // step, body, 0)
 
-    def send_part(k, l):
+    def send_part(k, l, h):
         return pltpu.make_async_remote_copy(
-            src_ref=outgoing.at[k, l],
-            dst_ref=heard.at[kind, k, l],
-            send_sem=part_sem.at[0, k, l],
-            recv_sem=part_sem.at[1 + kind, k, l],
+            src_ref=outgoing.at[k, l, h],
+            dst_ref=heard.at[kind, k, l, h],
+            send_sem=part_sem.at[0, k, l, h],
+            recv_sem=part_sem.at[1 + kind, k, l, h],
             device_id=(me_layer, me_feat, forward),
             device_id_type=MESH,
         )
 
-    def wait_part(which, k, l):
-        some = heard.at[which, k, l]
-        pltpu.make_async_copy(some, some, part_sem.at[1 + which, k, l]).wait()
-
-    def send_act(k, l):
+    def wait_part(which, k, l, h):
+        some = heard.at[which, k, l, h]
+        pltpu.make_async_copy(some, some, part_sem.at[1 + which, k, l, h]).wait()
+
+    def send_act(k, l, h):
         return pltpu.make_async_remote_copy(
-            src_ref=act_wire.at[k, l],
-            dst_ref=act_wire.at[k, l],
-            send_sem=act_sem.at[0, k, l],
-            recv_sem=act_sem.at[1, k, l],
+            src_ref=act_wire.at[k, l, h],
+            dst_ref=act_wire.at[k, l, h],
+            send_sem=act_sem.at[0, k, l, h],
+            recv_sem=act_sem.at[1, k, l, h],
             device_id=(me_layer, me_feat, outer),
             device_id_type=MESH,
         )
@@ -223,60 +227,71 @@
             load_enc[l].wait()
         first = ((y + k) % SIDE) * CORES
         some = rows[pl.ds(first, CORES), l].reshape(chunk_rows, -1)
-        partial = jnp.dot(some, ew[l], preferred_element_type=F32)
-
-        @pl.when(is_end)
-        def _():
-            outgoing[k, l] = to_wire(partial)
-            send_part(k, l).start()
-
-        @pl.when(is_mid)
-        def _():
-            part[k, l] = partial
+        for h in range(PIECES):
+            weights = ew[l, :, h * wide : (h + 1) * wide]
+            partial = jnp.dot(some, weights, preferred_element_type=F32)
+
+            @pl.when(is_end)
+            def _(h=h, partial=partial):
+                outgoing[k, l, h] = to_wire(partial)
+                send_part(k, l, h).start()
+
+            @pl.when(is_mid)
+            def _(h=h, partial=partial):
+                part[k, l, h] = partial
 
     def pass_on(k, l):
         @pl.when(is_mid)
         def _():
-            wait_part(0, k, l)
-            summed = part[k, l] + from_wire(heard[0, k, l])
-            outgoing[k, l] = to_wire(summed)
-            send_part(k, l).start()
-            part[k, l] = summed
+            for h in range(PIECES):
+                wait_part(0, k, l, h)
+                summed = part[k, l, h] + from_wire(heard[0, k, l, h])
+                outgoing[k, l, h] = to_wire(summed)
+                send_part(k, l, h).start()
+                part[k, l, h] = summed
 
     def finish(k, l):
-        @pl.when(is_mid)
-        def _():
-            wait_part(1, k, l)
-            pre = part[k, l] + from_wire(heard[1, k, l]) + eb[l : l + 1, :]
-            pre = jnp.maximum(pre, 0.0)
-            act_wire[k, l] = to_wire(pre)
-            send_act(k, l).start()
-            act[...] = pre
-
-        @pl.when(is_end)
-        def _():
-            some = act_wire.at[k, l]
-            pltpu.make_async_copy(some, some, act_sem.at[1, k, l]).wait()
-            act[...] = from_wire(act_wire[k, l])
-
-        decode(k, l)
-
-    def decode(k, l):
-        whole = act[...]
-        high = whole.astype(BF16)
-        low = (whole - high.astype(F32)).astype(BF16)
-        both = jnp.concatenate([high, low], axis=0)
+        terms = {}
+        for h in range(PIECES):
+
+            @pl.when(is_mid)
+            def _(h=h):
+                wait_part(1, k, l, h)
+                bias = eb[l : l + 1, h * wide : (h + 1) * wide]
+                pre = part[k, l, h] + from_wire(heard[1, k, l, h]) + bias
+                pre = jnp.maximum(pre, 0.0)
+                act_wire[k, l, h] = to_wire(pre)
+                send_act(k, l, h).start()
+                act[h] = pre
+
+            @pl.when(is_end)
+            def _(h=h):
+                some = act_wire.at[k, l, h]
+                pltpu.make_async_copy(some, some, act_sem.at[1, k, l, h]).wait()
+                act[h] = from_wire(act_wire[k, l, h])
+
+            decode(l, h, terms)
         for m in range(l, layers):
-            b = block_of(m, l)
-            twice = jnp.dot(both, dw_hi[b], preferred_element_type=F32)
-            term = twice[:chunk_rows] + twice[chunk_rows:]
-            term += jnp.dot(high, dw_lo[b], preferred_element_type=F32)
+            term = terms[m]
             if l > 0:
                 term += total[k, m]
             if m == l:
                 start_plane(k, m, term)
             else:
                 total[k, m] = term
+
+    def decode(l, h, terms):
+        whole = act[h]
+        high = whole.astype(BF16)
+        low = (whole - high.astype(F32)).astype(BF16)
+        both = jnp.concatenate([high, low], axis=0)
+        at = slice(h * wide, (h + 1) * wide)
+        for m in range(l, layers):
+            b = block_of(m, l)
+            twice = jnp.dot(both, dw_hi[b, at, :], preferred_element_type=F32)
+            term = twice[:chunk_rows] + twice[chunk_rows:]
+            term += jnp.dot(high, dw_lo[b, at, :], preferred_element_type=F32)
+            terms[m] = terms[m] + term if m in terms else term
 
     mine = me_layer * SIDE + x
     own_plane = [
@@ -301,15 +316,15 @@
                     pltpu.make_async_remote_copy(
                         src_ref=pair.at[k, m, to_core, to_x],
                         dst_ref=plane_in.at[mine, m],
-                        send_sem=plane_sem.at[0],
-                        recv_sem=plane_sem.at[1],
+                        send_sem=plane_sem.at[0, m],
+                        recv_sem=plane_sem.at[1, m],
                         device_id=(to_layer, deep * SIDE + to_x, me_width),
                         device_id_type=MESH,
                     ).start()
 
-    def plane_wait(way):
-        some = plane_in.at[pl.ds(0, group * SIDE - 1)]
-        pltpu.make_async_copy(some, some, plane_sem.at[way]).wait()
+    def plane_wait(way, m):
+        some = plane_in.at[pl.ds(0, group * SIDE - 1), m]
+        pltpu.make_async_copy(some, some, plane_sem.at[way, m]).wait()
 
     def send_ring(e):
         to_deep, to_width = (deep + e // SIDE) % SIDE, (me_width + e % SIDE) % SIDE
@@ -382,11 +397,10 @@
 
     for m in range(layers):
         own_plane[m].wait()
-    plane_wait(1)
-    summed = jnp.sum(plane_in[...], axis=0)
-    for to in range(SIDE):
-        for m in range(layers):
-            plane[to, m : m + 1, :] = summed[m, to : to + 1, :]
+        plane_wait(1, m)
+        summed = jnp.sum(plane_in[:, m], axis=0)
+        for to in range(SIDE):
+            plane[to, m : m + 1, :] = summed[to : to + 1, :]
     for e in (8, 9, 10, 11, 4, 12, 5, 6, 7, 13, 14, 15, 1, 2, 3):
         send_ring(e).start()
     deep_in[deep * SIDE + me_width] = plane[deep]
@@ -413,16 +427,18 @@
     recon[0:layers, :] = whole
 
     gather_sent()
-    plane_wait(0)
+    for m in range(layers):
+        plane_wait(0, m)
     ring_wait(0)
     for d in range(1, SIDE):
         send_side(d).wait_send()
     for k, l in ORDER:
-        send_part(k, l).wait_send()
-
-        @pl.when(is_mid)
-        def _(k=k, l=l):
-            send_act(k, l).wait_send()
+        for h in range(PIECES):
+            send_part(k, l, h).wait_send()
+
+            @pl.when(is_mid)
+            def _(k=k, l=l, h=h):
+                send_act(k, l, h).wait_send()
 
 
 def divide(layers, both, recon, err):
@@ -437,6 +453,7 @@
     blocks, _, width = dec_w.shape
     group = SIDE * CORES
     chunk_rows = CORES * own_rows
+    piece = (PIECES, chunk_rows, features // PIECES)
     vm = pltpu.VMEM
     dma = pltpu.SemaphoreType.DMA
     in_hbm = pl.BlockSpec(memory_space=pltpu.HBM)
@@ -456,11 +473,11 @@
             vm((blocks, features, width), BF16),
             vm((layers, width), F32),
             vm((layers, 1, width), F32),
-            vm((SIDE, layers, chunk_rows, features), F32),
-            vm((SIDE, layers, chunk_rows, features), WIRE),
-            vm((2, SIDE, layers, chunk_rows, features), WIRE),
-            vm((SIDE, layers, chunk_rows, features), WIRE),
-            vm((chunk_rows, features), F32),
+            vm((SIDE, layers) + piece, F32),
+            vm((SIDE, layers) + piece, WIRE),
+            vm((2, SIDE, layers) + piece, WIRE),
+            vm((SIDE, layers) + piece, WIRE),
+            vm(piece, F32),
             vm((SIDE, layers, chunk_rows, width), F32),
             vm((SIDE, layers, CORES, SIDE, SIDE, width), F32),
             vm((group * SIDE, layers, SIDE, width), F32),
@@ -471,9 +488,9 @@
             dma((layers,)),
             dma((blocks,)),
             dma((2, SIDE, layers)),
-            dma((3, SIDE, layers)),
-            dma((2, SIDE, layers)),
-            dma((2,)),
+            dma((3, SIDE, layers, PIECES)),
+            dma((2, SIDE, layers, PIECES)),
+            dma((2, layers)),
             dma((layers,)),
             dma((2,)),
             dma((2, SIDE)),

time: 44.3 us -> 44.1 us (level)
  no operation moved by 1% of the time
where the time goes in v6:
time: 44.1 us; the launch traced here: 44 us
  Pallas kernels  43.3 us (98%)
  between operations  0.64 us (1%)
    pallas_call x1, Pallas kernels, per_device(): pl.pallas_call(functools.partial(kernel, layers), out_shape=pltpu.VMEM((l...  42.7 us

profile of v6, /device:TPU:1, one launch (start us, length us, event | category | flops | bytes accessed | tf_op | source)
XLA Modules:
  0.0 44.0 jit_solution(1900811337625970505)
XLA Ops:
  0.6 42.7 %shard_map.77.both = f32[3,512]{1,0:T(4,128)S(1)} custom-call(bf16[2,16,512]{2,1,0:T(8,128)(2,1)} %resid.1, bf16[2,512,512]{2,1,0:T(8,128)(2,1)} %enc_w.1, f32[2,512]{1,0:T(2,128)} %enc_b.1, f32[3,512,512]{2,1,0:T(8,128)} %dec_w.1, f32[2,512]{1,0:T(2,128)} %dec_b.1, f32[2,1,512]{2,1,0:T(1,128)} %target.1), custom_call_target="tpu_custom_call" | custom-call | flops 1400000000 | bytes 4500000 | tf_op jit(solution)/shard_map/pallas_call | solution.py:461
  43.4 0.6 %shard_map.78 = (f32[2,1,512]{2,1,0:T(1,128)}, f32[1,2]{1,0:T(1,128)}) custom-call(f32[3,512]{1,0:T(4,128)S(1)} %shard_map.77.both), custom_call_target="tpu_custom_call" | custom-call | tf_op jit(solution)/shard_map/pallas_call | solution.py:506
